TPU v7x, 32 devices: a whole 2x2x4 slice. The times are simulated.
32 devices in a mesh: dp: 32 (over z, y, x, core).
Axes of the slice: x: 2, y: 2, z: 4, core: 2. Of those that a mesh axis runs over, the one named last changes fastest.
Arguments:
- tokens: bfloat16 [65536, 512], P('dp'), may hold values from -6 to 6
- segment: int32 [65536], P('dp'), may hold values from 0 to 2, as said below
- counts: int32 [32], P('dp'), may hold values from 1024 to 2048, as said below
- memory: bfloat16 [20, 512], P(None, 'dp'), may hold values from -6 to 6
- w_query: bfloat16 [512, 512], P('dp'), may hold values from -0.375 to 0.375
- b_query: bfloat16 [512], P('dp'), may hold values from -3 to 3
- w_key: bfloat16 [512, 512], P('dp'), may hold values from -0.25 to 0.25
- w_value: bfloat16 [512, 512], P('dp'), may hold values from -0.25 to 0.25
- b_value: bfloat16 [512], P('dp'), may hold values from -3 to 3
- w_out: bfloat16 [512, 512], P('dp'), may hold values from -1 to 1
- b_out: bfloat16 [512], P('dp'), may hold values from -3 to 3
- gain_attn: bfloat16 [512], P('dp'), may hold values from 0.5 to 1.5
- shift_attn: bfloat16 [512], P('dp'), may hold values from -3 to 3
- w_up: bfloat16 [512, 2048], P('dp'), may hold values from -0.25 to 0.25
- b_up: bfloat16 [2048], P('dp'), may hold values from -3 to 3
- w_down: bfloat16 [2048, 512], P('dp'), may hold values from -0.125 to 0.125
- b_down: bfloat16 [512], P('dp'), may hold values from -3 to 3
- gain_ffn: bfloat16 [512], P('dp'), may hold values from 0.5 to 1.5
- shift_ffn: bfloat16 [512], P('dp'), may hold values from -3 to 3
- cotangent: bfloat16 [65536, 512], P('dp'), may hold values from -6 to 6
Outputs:
- output: bfloat16 [65536, 512], P('dp')
- grad_tokens: float32 [65536, 512], P('dp')
- grad_memory: float32 [20, 512], P(None, 'dp')
- grad_w_query: float32 [512, 512], P('dp')
- grad_b_query: float32 [512], P('dp')
- grad_w_key: float32 [512, 512], P('dp')
- grad_w_value: float32 [512, 512], P('dp')
- grad_b_value: float32 [512], P('dp')
- grad_w_out: float32 [512, 512], P('dp')
- grad_b_out: float32 [512], P('dp')
- grad_gain_attn: float32 [512], P('dp')
- grad_shift_attn: float32 [512], P('dp')
- grad_w_up: float32 [512, 2048], P('dp')
- grad_b_up: float32 [2048], P('dp')
- grad_w_down: float32 [2048, 512], P('dp')
- grad_b_down: float32 [512], P('dp')
- grad_gain_ffn: float32 [512], P('dp')
- grad_shift_ffn: float32 [512], P('dp')
Inputs may be any that keep to these rules, and one draw needn't show every extreme that they name: `segment`: within each device's 2048 slots the ids never fall and each id marks one sequence; every used sequence has 128 to 1024 slots; in every draw some device holds a used sequence of exactly 1024 tokens. Ids past a device's used count carry no meaning. `counts`: slots are used from the start of each device and end where a sequence ends; in every draw some device uses all 2048 and some device uses 1024.
All inputs are finite; a program needn't handle non-finite values.
Results may differ from a plain program's by a relative error of at most 0.015.
The roundings to bfloat16 on the way count: a program that leaves them out, or rounds other values in their place, can miss the bound.
Values may be sent and summed in bfloat16 or wider, within the bound.
A program may use at most 320 MiB of HBM per device.

v0:
```python
import jax
import jax.numpy as jnp
from jax import lax
from jax.sharding import PartitionSpec as P

H = 8
HD = 64
QB = 512
EPS = 1e-05
NEG = -1e30


def normalize(value, gain):
    mean = jnp.mean(value, axis=-1, keepdims=True)
    centred = value - mean
    spread = jnp.mean(centred * centred, axis=-1, keepdims=True)
    return centred * lax.rsqrt(spread + EPS) * gain


def smooth(value):
    return jax.nn.gelu(value, approximate=False)


def matmul(left, right):
    return jnp.dot(left, right, preferred_element_type=jnp.float32)


def grad_weight(left, right):
    return lax.dot_general(
        left, right, (((0,), (0,)), ((), ())), preferred_element_type=jnp.float32
    )


def grad_input(left, right):
    return lax.dot_general(
        left, right, (((1,), (1,)), ((), ())), preferred_element_type=jnp.float32
    )


def column_sum(value):
    return jnp.sum(value.astype(jnp.float32), axis=0)


def shards(
    tokens,
    segment,
    counts,
    memory,
    w_query,
    b_query,
    w_key,
    w_value,
    b_value,
    w_out,
    b_out,
    gain_attn,
    shift_attn,
    w_up,
    b_up,
    w_down,
    b_down,
    gain_ffn,
    shift_ffn,
    cotangent,
):
    full = (
        lax.all_gather(memory, "dp", axis=1, tiled=True),
        lax.all_gather(w_query, "dp", axis=0, tiled=True),
        lax.all_gather(b_query, "dp", axis=0, tiled=True),
        lax.all_gather(w_key, "dp", axis=0, tiled=True),
        lax.all_gather(w_value, "dp", axis=0, tiled=True),
        lax.all_gather(b_value, "dp", axis=0, tiled=True),
        lax.all_gather(w_out, "dp", axis=0, tiled=True),
        lax.all_gather(b_out, "dp", axis=0, tiled=True),
        lax.all_gather(gain_attn, "dp", axis=0, tiled=True),
        lax.all_gather(shift_attn, "dp", axis=0, tiled=True),
        lax.all_gather(w_up, "dp", axis=0, tiled=True),
        lax.all_gather(b_up, "dp", axis=0, tiled=True),
        lax.all_gather(w_down, "dp", axis=0, tiled=True),
        lax.all_gather(b_down, "dp", axis=0, tiled=True),
        lax.all_gather(gain_ffn, "dp", axis=0, tiled=True),
        lax.all_gather(shift_ffn, "dp", axis=0, tiled=True),
    )
    (
        memory_full,
        query_weight,
        query_bias,
        key_weight,
        value_weight,
        value_bias,
        out_weight,
        out_bias,
        gain_one,
        shift_one,
        up_weight,
        up_bias,
        down_weight,
        down_bias,
        gain_two,
        shift_two,
    ) = full
    slots = tokens.shape[0]
    width = tokens.shape[1]
    memory_rows = memory_full.shape[0]
    blocks = slots // QB
    scale = HD ** (-0.5)
    valid = jnp.arange(slots) < counts[0]
    key_seg = jnp.where(valid, segment, -1)
    queries = (matmul(tokens, query_weight) + query_bias.astype(jnp.float32)).astype(jnp.bfloat16)
    keys_tok = matmul(tokens, key_weight).astype(jnp.bfloat16)
    keys_mem = matmul(memory_full, key_weight).astype(jnp.bfloat16)
    values_tok = (matmul(tokens, value_weight) + value_bias.astype(jnp.float32)).astype(
        jnp.bfloat16
    )
    values_mem = (matmul(memory_full, value_weight) + value_bias.astype(jnp.float32)).astype(
        jnp.bfloat16
    )
    key_heads = keys_tok.reshape(slots, H, HD)
    key_mem_heads = keys_mem.reshape(memory_rows, H, HD)
    value_heads = values_tok.reshape(slots, H, HD)
    value_mem_heads = values_mem.reshape(memory_rows, H, HD)
    query_blocks = queries.reshape(blocks, QB, H, HD)
    seg_blocks = segment.reshape(blocks, QB)

    def score_block(query_block, seg_block):
        tok_scores = (
            jnp.einsum("qhd,khd->hqk", query_block, key_heads, preferred_element_type=jnp.float32)
            * scale
        )
        mem_scores = (
            jnp.einsum(
                "qhd,khd->hqk", query_block, key_mem_heads, preferred_element_type=jnp.float32
            )
            * scale
        )
        allowed = key_seg[None, :] == seg_block[:, None]
        return (jnp.where(allowed[None], tok_scores, NEG), mem_scores)

    def forward_block(item):
        query_block, seg_block = item
        tok_scores, mem_scores = score_block(query_block, seg_block)
        top = jnp.maximum(jnp.max(tok_scores, axis=-1), jnp.max(mem_scores, axis=-1))
        tok_exp = jnp.exp(tok_scores - top[..., None])
        mem_exp = jnp.exp(mem_scores - top[..., None])
        total = jnp.sum(tok_exp, axis=-1) + jnp.sum(mem_exp, axis=-1)
        tok_weights = (tok_exp / total[..., None]).astype(jnp.bfloat16)
        mem_weights = (mem_exp / total[..., None]).astype(jnp.bfloat16)
        mixed_block = jnp.einsum(
            "hqk,khd->qhd", tok_weights, value_heads, preferred_element_type=jnp.float32
        )
        mixed_block = mixed_block + jnp.einsum(
            "hqk,khd->qhd", mem_weights, value_mem_heads, preferred_element_type=jnp.float32
        )
        return (mixed_block.astype(jnp.bfloat16), top + jnp.log(total))

    mixed_blocks, log_totals = lax.map(forward_block, (query_blocks, seg_blocks))
    mixed = mixed_blocks.reshape(slots, width)
    attention = matmul(mixed, out_weight) + out_bias.astype(jnp.float32)
    first_sum = tokens.astype(jnp.float32) + attention
    first = normalize(first_sum, gain_one.astype(jnp.float32)) + shift_one.astype(jnp.float32)
    first_low = first.astype(jnp.bfloat16)
    hidden = matmul(first_low, up_weight) + up_bias.astype(jnp.float32)
    active = smooth(hidden).astype(jnp.bfloat16)
    branch = matmul(active, down_weight) + down_bias.astype(jnp.float32)
    second_sum = first + branch
    result = normalize(second_sum, gain_two.astype(jnp.float32)) + shift_two.astype(jnp.float32)
    output = jnp.where(valid[:, None], result, 0.0).astype(jnp.bfloat16)
    again = (
        lax.all_gather(memory, "dp", axis=1, tiled=True),
        lax.all_gather(w_query, "dp", axis=0, tiled=True),
        lax.all_gather(w_key, "dp", axis=0, tiled=True),
        lax.all_gather(w_value, "dp", axis=0, tiled=True),
        lax.all_gather(w_out, "dp", axis=0, tiled=True),
        lax.all_gather(w_up, "dp", axis=0, tiled=True),
        lax.all_gather(w_down, "dp", axis=0, tiled=True),
        lax.all_gather(gain_attn, "dp", axis=0, tiled=True),
        lax.all_gather(gain_ffn, "dp", axis=0, tiled=True),
    )
    (
        memory_back,
        query_back,
        key_back,
        value_back,
        out_back,
        up_back,
        down_back,
        gain_one_back,
        gain_two_back,
    ) = again
    seed_grad = jnp.where(valid[:, None], cotangent.astype(jnp.float32), 0.0)
    unused_two, second_back = jax.vjp(normalize, second_sum, gain_two_back.astype(jnp.float32))
    grad_second, grad_gain_two = second_back(seed_grad)
    grad_shift_two = jnp.sum(seed_grad, axis=0)
    branch_grad = grad_second.astype(jnp.bfloat16)
    grad_down = grad_weight(active, branch_grad)
    grad_down_bias = column_sum(branch_grad)
    active_grad = grad_input(branch_grad, down_back)
    unused_hidden, smooth_back = jax.vjp(smooth, hidden)
    hidden_grad = smooth_back(active_grad)[0].astype(jnp.bfloat16)
    grad_up = grad_weight(first_low, hidden_grad)
    grad_up_bias = column_sum(hidden_grad)
    first_grad = grad_second + grad_input(hidden_grad, up_back)
    unused_one, first_back = jax.vjp(normalize, first_sum, gain_one_back.astype(jnp.float32))
    grad_first_sum, grad_gain_one = first_back(first_grad)
    grad_shift_one = jnp.sum(first_grad, axis=0)
    attention_grad = grad_first_sum.astype(jnp.bfloat16)
    grad_out = grad_weight(mixed, attention_grad)
    grad_out_bias = column_sum(attention_grad)
    mixed_grad = grad_input(attention_grad, out_back).astype(jnp.bfloat16)
    grad_blocks = mixed_grad.reshape(blocks, QB, H, HD)

    def backward_block(carry, item):
        key_tok_acc, value_tok_acc, key_mem_acc, value_mem_acc = carry
        query_block, grad_block, total_block, seg_block = item
        tok_scores, mem_scores = score_block(query_block, seg_block)
        tok_probs = jnp.exp(tok_scores - total_block[..., None])
        mem_probs = jnp.exp(mem_scores - total_block[..., None])
        tok_dprobs = jnp.einsum(
            "qhd,khd->hqk", grad_block, value_heads, preferred_element_type=jnp.float32
        )
        mem_dprobs = jnp.einsum(
            "qhd,khd->hqk", grad_block, value_mem_heads, preferred_element_type=jnp.float32
        )
        centre = jnp.sum(tok_probs * tok_dprobs, axis=-1) + jnp.sum(mem_probs * mem_dprobs, axis=-1)
        tok_sgrad = (tok_probs * (tok_dprobs - centre[..., None])).astype(jnp.bfloat16)
        mem_sgrad = (mem_probs * (mem_dprobs - centre[..., None])).astype(jnp.bfloat16)
        query_part = jnp.einsum(
            "hqk,khd->qhd", tok_sgrad, key_heads, preferred_element_type=jnp.float32
        )
        query_part = (
            query_part
            + jnp.einsum(
                "hqk,khd->qhd", mem_sgrad, key_mem_heads, preferred_element_type=jnp.float32
            )
        ) * scale
        key_tok_acc = (
            key_tok_acc
            + jnp.einsum("hqk,qhd->khd", tok_sgrad, query_block, preferred_element_type=jnp.float32)
            * scale
        )
        key_mem_acc = (
            key_mem_acc
            + jnp.einsum("hqk,qhd->khd", mem_sgrad, query_block, preferred_element_type=jnp.float32)
            * scale
        )
        value_tok_acc = value_tok_acc + jnp.einsum(
            "hqk,qhd->khd",
            tok_probs.astype(jnp.bfloat16),
            grad_block,
            preferred_element_type=jnp.float32,
        )
        value_mem_acc = value_mem_acc + jnp.einsum(
            "hqk,qhd->khd",
            mem_probs.astype(jnp.bfloat16),
            grad_block,
            preferred_element_type=jnp.float32,
        )
        return (
            (key_tok_acc, value_tok_acc, key_mem_acc, value_mem_acc),
            query_part.astype(jnp.bfloat16),
        )

    start = (
        jnp.zeros((slots, H, HD), jnp.float32),
        jnp.zeros((slots, H, HD), jnp.float32),
        jnp.zeros((memory_rows, H, HD), jnp.float32),
        jnp.zeros((memory_rows, H, HD), jnp.float32),
    )
    sums, query_parts = lax.scan(
        backward_block, start, (query_blocks, grad_blocks, log_totals, seg_blocks)
    )
    key_tok_grad = sums[0].reshape(slots, width).astype(jnp.bfloat16)
    value_tok_grad = sums[1].reshape(slots, width).astype(jnp.bfloat16)
    key_mem_grad = sums[2].reshape(memory_rows, width).astype(jnp.bfloat16)
    value_mem_grad = sums[3].reshape(memory_rows, width).astype(jnp.bfloat16)
    query_grad = query_parts.reshape(slots, width)
    grad_query = grad_weight(tokens, query_grad)
    grad_query_bias = column_sum(query_grad)
    grad_key = grad_weight(tokens, key_tok_grad) + grad_weight(memory_back, key_mem_grad)
    grad_value = grad_weight(tokens, value_tok_grad) + grad_weight(memory_back, value_mem_grad)
    grad_value_bias = column_sum(value_tok_grad) + column_sum(value_mem_grad)
    grad_memory = grad_input(key_mem_grad, key_back) + grad_input(value_mem_grad, value_back)
    grad_tokens = grad_first_sum + grad_input(query_grad, query_back)
    grad_tokens = (
        grad_tokens + grad_input(key_tok_grad, key_back) + grad_input(value_tok_grad, value_back)
    )
    owned = (
        lax.psum_scatter(grad_memory, "dp", scatter_dimension=1, tiled=True),
        lax.psum_scatter(grad_query, "dp", scatter_dimension=0, tiled=True),
        lax.psum_scatter(grad_query_bias, "dp", scatter_dimension=0, tiled=True),
        lax.psum_scatter(grad_key, "dp", scatter_dimension=0, tiled=True),
        lax.psum_scatter(grad_value, "dp", scatter_dimension=0, tiled=True),
        lax.psum_scatter(grad_value_bias, "dp", scatter_dimension=0, tiled=True),
        lax.psum_scatter(grad_out, "dp", scatter_dimension=0, tiled=True),
        lax.psum_scatter(grad_out_bias, "dp", scatter_dimension=0, tiled=True),
        lax.psum_scatter(grad_gain_one, "dp", scatter_dimension=0, tiled=True),
        lax.psum_scatter(grad_shift_one, "dp", scatter_dimension=0, tiled=True),
        lax.psum_scatter(grad_up, "dp", scatter_dimension=0, tiled=True),
        lax.psum_scatter(grad_up_bias, "dp", scatter_dimension=0, tiled=True),
        lax.psum_scatter(grad_down, "dp", scatter_dimension=0, tiled=True),
        lax.psum_scatter(grad_down_bias, "dp", scatter_dimension=0, tiled=True),
        lax.psum_scatter(grad_gain_two, "dp", scatter_dimension=0, tiled=True),
        lax.psum_scatter(grad_shift_two, "dp", scatter_dimension=0, tiled=True),
    )
    return (
        output,
        grad_tokens,
        owned[0],
        owned[1],
        owned[2],
        owned[3],
        owned[4],
        owned[5],
        owned[6],
        owned[7],
        owned[8],
        owned[9],
        owned[10],
        owned[11],
        owned[12],
        owned[13],
        owned[14],
        owned[15],
    )


def solution(mesh):
    in_specs = (
        P("dp", None),
        P("dp"),
        P("dp"),
        P(None, "dp"),
        P("dp", None),
        P("dp"),
        P("dp", None),
        P("dp", None),
        P("dp"),
        P("dp", None),
        P("dp"),
        P("dp"),
        P("dp"),
        P("dp", None),
        P("dp"),
        P("dp", None),
        P("dp"),
        P("dp"),
        P("dp"),
        P("dp", None),
    )
    out_specs = (
        P("dp", None),
        P("dp", None),
        P(None, "dp"),
        P("dp", None),
        P("dp"),
        P("dp", None),
        P("dp", None),
        P("dp"),
        P("dp", None),
        P("dp"),
        P("dp"),
        P("dp"),
        P("dp", None),
        P("dp"),
        P("dp", None),
        P("dp"),
        P("dp"),
        P("dp"),
    )
    return jax.shard_map(shards, mesh=mesh, in_specs=in_specs, out_specs=out_specs, check_vma=False)
```

profile of v0, /device:TPU:0, one launch (start us, length us, event | category | flops | bytes accessed | tf_op | source)
XLA Modules:
  0.0 2035.3 jit_solution(17654876365592954387)
XLA Ops:
  16.4 42.2 %all-reduce.19 = (bf16[512]{0:T(512)(128)(2,1)S(1)}, bf16[512]{0:T(512)(128)(2,1)S(1)}, bf16[512]{0:T(512)(128)(2,1)S(1)}, bf16[512]{0:T(512)(128)(2,1)S(1)}, bf...) all-reduce(bf16[512]{0:T(512)(128)(2,1)S(1)} %dynamic-update-slice,, ...), channel_id=1, replica_groups=mesh['dp'=32] {'dp'}, use_global_device_ids=true, to_apply=%add | all-reduce | flops 6144 | bytes 24576
  58.6 41.0 %all_gather.60 = bf16[20,512]{0,1:T(8,128)(2,1)S(1)} all-gather(bf16[20,16]{0,1:T(8,128)(2,1)} %param.27), channel_id=1, replica_groups=mesh['dp'=32] {'dp'}, dimensions={1}, use_global_device_ids=true | all-gather | bytes 21120 | tf_op jit(solution)/shard_map/all_gather | solution.py:67
  99.6 38.9 %all_gather.59 = bf16[512,512]{1,0:T(8,128)(2,1)S(1)} all-gather(bf16[16,512]{1,0:T(8,128)(2,1)} %param.30), channel_id=1, replica_groups=mesh['dp'=32] {'dp'}, dimensions={0}, use_global_device_ids=true | all-gather | bytes 540672 | tf_op jit(solution)/shard_map/all_gather | solution.py:70
  138.5 39.5 %all_gather.61 = bf16[512,512]{1,0:T(8,128)(2,1)S(1)} all-gather(bf16[16,512]{1,0:T(8,128)(2,1)} %param.31), channel_id=1, replica_groups=mesh['dp'=32] {'dp'}, dimensions={0}, use_global_device_ids=true | all-gather | bytes 540672 | tf_op jit(solution)/shard_map/all_gather | solution.py:71
  196.1 38.2 %all_gather.57 = bf16[512,512]{1,0:T(8,128)(2,1)S(1)} all-gather(bf16[16,512]{1,0:T(8,128)(2,1)S(1)} %copy-done.48), channel_id=1, replica_groups=mesh['dp'=32] {'dp'}, dimensions={0}, use_global_device_ids=true | all-gather | bytes 540672 | tf_op jit(solution)/shard_map/all_gather | solution.py:68
  234.3 42.2 %all_gather.63 = bf16[512,512]{1,0:T(8,128)(2,1)} all-gather(bf16[16,512]{1,0:T(8,128)(2,1)S(1)} %copy-done.49), channel_id=1, replica_groups=mesh['dp'=32] {'dp'}, dimensions={0}, use_global_device_ids=true | all-gather | bytes 540672 | tf_op jit(solution)/shard_map/all_gather | solution.py:73
  284.6 6.1 reshape.285
  290.7 5.4 copy.82
  297.7 208.1 %while.31 = (s32[]{:T(128)}, bf16[4,512,8,64]{1,3,2,0:T(8,128)(2,1)}, f32[4,8,512]{2,1,0:T(8,128)}, s32[2048]{0:T(1024)}, s32[4,512]{1,0:T(4,128)}, /*index=5*/b...) while((s32[]{:T(128)}, ...), condition=%wide.region_5.6_spmd, body=%wide.region_0.5_spmd.sunk | while | flops 2271260672 | bytes 114112640 | solution.py:156
  301.0 14.8 fusion.188
  315.9 15.0 fusion.190
  331.5 15.7 fusion.192
  352.9 14.8 fusion.188
  367.8 15.0 fusion.190
  383.4 15.7 fusion.192
  404.8 14.8 fusion.188
  419.7 15.0 fusion.190
  435.3 15.7 fusion.192
  456.8 14.8 fusion.188
  471.6 15.0 fusion.190
  487.2 15.7 fusion.192
  515.2 46.5 %multiply_convert_fusion.2 = (bf16[2048,2048]{1,0:T(8,128)(2,1)}, f32[2048,2048]{1,0:T(8,128)}, f32[2048,2048]{1,0:T(8,128)}) fusion(f32[2048]{0:T(1024)S(1)} %copy-done.56, bf16[512,2048]{1,0:T(8,128)(2,1)} %all-gather.3.cloned.1.call-done, f32[2048,512]{0,1:T(8,128)} %copy-done.10, f32[512]{0:T(512)S(1)} %copy-done.61, f32[512]{0:T(512)S(1)} %copy-done.57, ...), kind=kOutput, calls=%fused_computation.84 | convolution fusion | flops 4577034240 | bytes 48263168 | tf_op jit(solution)/shard_map/dot_general | solution.py:25
  561.9 11.1 fusion.81
  577.7 4.8 convert_reduce_fusion.1
  582.5 22.8 %convert_reduce_fusion = (f32[2048]{0:T(1024)}, bf16[2048,2048]{1,0:T(8,128)(2,1)}) fusion(f32[2048,2048]{1,0:T(8,128)} %get-tuple-element.425, bf16[2048,512]{0,1:T(8,128)(2,1)} %get-tuple-element.415, bf16[2048,512]{1,0:T(8,128)(2,1)} %all-gather.5.cloned.1.call-done, f32[2048,2048]{1,0:T(8,128)} %get-tuple-element.439, f32[2048]{0:T(1024)S(1)} %copy-done.56), kind=kOutput, calls=%fused_computation.82 | convolution fusion | flops 4366268416 | bytes 46153728 | tf_op jit(solution)/shard_map/dot_general | solution.py:35
  605.2 12.9 multiply_reduce_fusion.3
  629.0 5.6 copy.90
  636.2 445.1 %while.32 = (s32[]{:T(128)}, f32[2048,8,64]{0,2,1:T(8,128)}, f32[2048,8,64]{0,2,1:T(8,128)}, f32[20,8,64]{2,0,1:T(8,128)S(1)}, f32[20,8,64]{2,0,1:T(8,128)S(1)},...) while((s32[]{:T(128)}, f32[2048,8,64]{0,2,1:T(8,128)}, ...), condition=%wide.region_17.18_spmd.clone, body=%wide.region_14.17_spmd.clone.sunk | while | flops 5504415744 | bytes 366266624 | solution.py:269
  643.2 14.1 fusion.212
  657.4 24.6 %multiply_reduce_fusion.10 = (f32[8,512]{1,0:T(8,128)S(1)}, f32[8,512,2048]{2,1,0:T(8,128)}) fusion(f32[8,512,2048]{2,1,0:T(8,128)} %fusion.212, f32[8,512]{1,0:T(8,128)S(1)} %dynamic-slice_bitcast_fusion.2, bf16[2048,8,64]{0,2,1:T(8,128)(2,1)S(1)} %get-tuple-element.693, bf16[4,512,8,64]{1,3,2,0:T(8,128)(2,1)} %get-tuple-element.690, ...), kind=kOutput, calls=%fused_computation.29.clone.1 | convolution fusion | flops 1115680768 | bytes 70811648 | tf_op jit(solution)/shard_map/while/body/eval_jaxpr/qhd,khd->hqk/dot_general | solution.py:127
  682.0 27.4 %multiply_convert_fusion.5 = bf16[8,512,2048]{2,1,0:T(8,128)(2,1)} fusion(f32[8,512,2048]{2,1,0:T(8,128)} %get-tuple-element.613, f32[8,512,2048]{2,1,0:T(8,128)} %fusion.212, f32[8,512]{1,0:T(8,128)S(1)} %add.399), kind=kLoop, calls=%fused_computation.28.clone.1 | loop fusion | flops 25165824 | bytes 83902464 | tf_op jit(solution)/shard_map/while/body/eval_jaxpr/convert_element_type | solution.py:225
  709.4 15.7 bitcast_add_fusion.5
  726.5 9.8 fusion.216
  737.5 6.3 bitcast_add_fusion.4
  752.5 14.2 fusion.212
  766.7 24.7 %multiply_reduce_fusion.10 = (f32[8,512]{1,0:T(8,128)S(1)}, f32[8,512,2048]{2,1,0:T(8,128)}) fusion(f32[8,512,2048]{2,1,0:T(8,128)} %fusion.212, f32[8,512]{1,0:T(8,128)S(1)} %dynamic-slice_bitcast_fusion.2, bf16[2048,8,64]{0,2,1:T(8,128)(2,1)S(1)} %get-tuple-element.693, bf16[4,512,8,64]{1,3,2,0:T(8,128)(2,1)} %get-tuple-element.690, ...), kind=kOutput, calls=%fused_computation.29.clone.1 | convolution fusion | flops 1115680768 | bytes 70811648 | tf_op jit(solution)/shard_map/while/body/eval_jaxpr/qhd,khd->hqk/dot_general | solution.py:127
  791.3 27.4 %multiply_convert_fusion.5 = bf16[8,512,2048]{2,1,0:T(8,128)(2,1)} fusion(f32[8,512,2048]{2,1,0:T(8,128)} %get-tuple-element.613, f32[8,512,2048]{2,1,0:T(8,128)} %fusion.212, f32[8,512]{1,0:T(8,128)S(1)} %add.399), kind=kLoop, calls=%fused_computation.28.clone.1 | loop fusion | flops 25165824 | bytes 83902464 | tf_op jit(solution)/shard_map/while/body/eval_jaxpr/convert_element_type | solution.py:225
  818.7 16.9 bitcast_add_fusion.5
  837.0 9.8 fusion.216
  847.9 7.6 bitcast_add_fusion.4
  864.3 14.2 fusion.212
  878.5 24.6 %multiply_reduce_fusion.10 = (f32[8,512]{1,0:T(8,128)S(1)}, f32[8,512,2048]{2,1,0:T(8,128)}) fusion(f32[8,512,2048]{2,1,0:T(8,128)} %fusion.212, f32[8,512]{1,0:T(8,128)S(1)} %dynamic-slice_bitcast_fusion.2, bf16[2048,8,64]{0,2,1:T(8,128)(2,1)S(1)} %get-tuple-element.693, bf16[4,512,8,64]{1,3,2,0:T(8,128)(2,1)} %get-tuple-element.690, ...), kind=kOutput, calls=%fused_computation.29.clone.1 | convolution fusion | flops 1115680768 | bytes 70811648 | tf_op jit(solution)/shard_map/while/body/eval_jaxpr/qhd,khd->hqk/dot_general | solution.py:127
  903.1 27.4 %multiply_convert_fusion.5 = bf16[8,512,2048]{2,1,0:T(8,128)(2,1)} fusion(f32[8,512,2048]{2,1,0:T(8,128)} %get-tuple-element.613, f32[8,512,2048]{2,1,0:T(8,128)} %fusion.212, f32[8,512]{1,0:T(8,128)S(1)} %add.399), kind=kLoop, calls=%fused_computation.28.clone.1 | loop fusion | flops 25165824 | bytes 83902464 | tf_op jit(solution)/shard_map/while/body/eval_jaxpr/convert_element_type | solution.py:225
  930.5 16.9 bitcast_add_fusion.5
  948.8 9.8 fusion.216
  959.7 7.6 bitcast_add_fusion.4
  976.1 14.1 fusion.212
  990.3 24.6 %multiply_reduce_fusion.10 = (f32[8,512]{1,0:T(8,128)S(1)}, f32[8,512,2048]{2,1,0:T(8,128)}) fusion(f32[8,512,2048]{2,1,0:T(8,128)} %fusion.212, f32[8,512]{1,0:T(8,128)S(1)} %dynamic-slice_bitcast_fusion.2, bf16[2048,8,64]{0,2,1:T(8,128)(2,1)S(1)} %get-tuple-element.693, bf16[4,512,8,64]{1,3,2,0:T(8,128)(2,1)} %get-tuple-element.690, ...), kind=kOutput, calls=%fused_computation.29.clone.1 | convolution fusion | flops 1115680768 | bytes 70811648 | tf_op jit(solution)/shard_map/while/body/eval_jaxpr/qhd,khd->hqk/dot_general | solution.py:127
  1014.9 27.4 %multiply_convert_fusion.5 = bf16[8,512,2048]{2,1,0:T(8,128)(2,1)} fusion(f32[8,512,2048]{2,1,0:T(8,128)} %get-tuple-element.613, f32[8,512,2048]{2,1,0:T(8,128)} %fusion.212, f32[8,512]{1,0:T(8,128)S(1)} %add.399), kind=kLoop, calls=%fused_computation.28.clone.1 | loop fusion | flops 25165824 | bytes 83902464 | tf_op jit(solution)/shard_map/while/body/eval_jaxpr/convert_element_type | solution.py:225
  1042.3 16.9 bitcast_add_fusion.5
  1060.6 9.8 fusion.216
  1071.5 7.6 bitcast_add_fusion.4
  1085.0 4.6 fusion.86
  1110.0 11.2 fusion.72
  1121.5 10.5 fusion.87
  1146.1 5.3 copy.100
  1151.5 37.4 %all-reduce.18 = (f32[512]{0:T(512)S(1)}, f32[512]{0:T(512)S(1)}, f32[512]{0:T(512)S(1)}, f32[512]{0:T(512)S(1)}, f32[512]{0:T(512)S(1)}, /*index=5*/f32[2048]{0...) all-reduce(f32[512]{0:T(512)S(1)} %reduce_sum.215, ...), channel_id=4, replica_groups=mesh['dp'=32] {'dp'}, use_global_device_ids=true, to_apply=%region_21.22.clone | all-reduce | flops 6144 | bytes 49152
  1194.1 20.8 %reduce-scatter.14.cloned.1.call-done = f32[20,16]{0,1:T(8,128)} async-done(((f32[20,512]{0,1:T(8,128)}), f32[20,16]{0,1:T(8,128)}) %reduce-scatter.14.cloned.1.call-update) | async-done | bytes 1296 | tf_op jit(solution)/shard_map/reduce_scatter | solution.py:288
  1214.9 133.5 %reduce-scatter.16.cloned.1.call-done = f32[16,512]{1,0:T(8,128)} async-done(((f32[512,512]{1,0:T(8,128)}), f32[16,512]{1,0:T(8,128)}) %reduce-scatter.16.cloned.1.call-update) | async-done | bytes 32784 | tf_op jit(solution)/shard_map/reduce_scatter | solution.py:294
  1348.3 133.4 %reduce-scatter.22.cloned.1.call-done = f32[16,512]{1,0:T(8,128)} async-done(((f32[512,512]{1,0:T(8,128)}), f32[16,512]{1,0:T(8,128)}) %reduce-scatter.22.cloned.1.call-update) | async-done | bytes 32784
  1481.8 133.5 %reduce-scatter.24.cloned.1.call-done = f32[16,512]{1,0:T(8,128)} async-done(((f32[512,512]{1,0:T(8,128)}), f32[16,512]{1,0:T(8,128)}) %reduce-scatter.24.cloned.1.call-update) | async-done | bytes 32784
  1615.3 133.6 %reduce-scatter.26.cloned.1.call-done = f32[16,512]{1,0:T(8,128)} async-done(((f32[512,512]{1,0:T(8,128)}), f32[16,512]{1,0:T(8,128)}) %reduce-scatter.26.cloned.1.call-update) | async-done | bytes 32784
  1748.8 139.7 %reduce-scatter.18.cloned.1.call-done = f32[16,2048]{1,0:T(8,128)} async-done(((f32[512,2048]{1,0:T(8,128)}), f32[16,2048]{1,0:T(8,128)}) %reduce-scatter.18.cloned.1.call-update) | async-done | bytes 131088 | tf_op jit(solution)/shard_map/reduce_scatter | solution.py:298
  1888.5 139.8 %reduce-scatter.20.cloned.1.call-done = f32[64,512]{1,0:T(8,128)} async-done(((f32[2048,512]{1,0:T(8,128)}), f32[64,512]{1,0:T(8,128)}) %reduce-scatter.20.cloned.1.call-update) | async-done | bytes 131088 | tf_op jit(solution)/shard_map/reduce_scatter | solution.py:300
  (338 shorter events, 176.2 us)
Async XLA Ops:
  7.2 508.0 %all-gather.3.cloned.1.call-start = ((), (), s32[]{:S(2)}) async-start(), calls=%async_computation.7 | async-start | bytes 2162688 | tf_op jit(solution)/shard_map/all_gather | solution.py:77
  7.9 553.9 %all-gather.5.cloned.1.call-start = ((), (), s32[]{:S(2)}) async-start(), calls=%async_computation.8 | async-start | bytes 2162688 | tf_op jit(solution)/shard_map/all_gather | solution.py:79
  8.7 1206.2 %reduce-scatter.14.cloned.1.call-start = ((), (), s32[]{:S(2)}) async-start(), calls=%async_computation.9 | async-start | bytes 270336 | tf_op jit(solution)/shard_map/reduce_scatter | solution.py:288
  99.6 78.6 %copy-start.23 = (bf16[20,512]{0,1:T(8,128)(2,1)}, bf16[20,512]{0,1:T(8,128)(2,1)S(1)}, u32[]{:S(2)}) copy-start(bf16[20,512]{0,1:T(8,128)(2,1)S(1)} %all_gather.60) | copy-start | bytes 61444
  138.5 44.3 %copy-start.19 = (bf16[512,512]{1,0:T(8,128)(2,1)}, bf16[512,512]{1,0:T(8,128)(2,1)S(1)}, u32[]{:S(2)}) copy-start(bf16[512,512]{1,0:T(8,128)(2,1)S(1)} %all_gather.59) | copy-start | bytes 1572868
  178.0 4.8 copy-start.13
  178.2 4.6 copy-start.26
  184.1 9.3 copy-start.45
  184.1 12.0 copy-start.48
  184.1 50.1 %copy-start.49 = (bf16[16,512]{1,0:T(8,128)(2,1)S(1)}, bf16[16,512]{1,0:T(8,128)(2,1)}, u32[]{:S(2)}) copy-start(bf16[16,512]{1,0:T(8,128)(2,1)} %param.33) | copy-start | bytes 49156
  234.3 50.3 %copy-start.32 = (bf16[512,512]{1,0:T(8,128)(2,1)}, bf16[512,512]{1,0:T(8,128)(2,1)S(1)}, u32[]{:S(2)}) copy-start(bf16[512,512]{1,0:T(8,128)(2,1)S(1)} %all_gather.57) | copy-start | bytes 1572868
  505.7 4.7 copy-start.1
  505.8 4.7 copy-start.31
  505.8 4.7 copy-start.35
  505.8 4.7 copy-start.64
  512.0 3.2 copy-start.56
  512.1 3.2 copy-start.57
  512.1 3.2 copy-start.61
  512.1 106.1 %copy-start.41 = (f32[2048]{0:T(1024)}, f32[2048]{0:T(1024)S(1)}, u32[]{:S(2)}) copy-start(f32[2048]{0:T(1024)S(1)} %broadcast_multiply_fusion.1) | copy-start | bytes 24580
  515.2 103.0 %copy-start.46 = (f32[2048]{0:T(1024)}, f32[2048]{0:T(1024)S(1)}, u32[]{:S(2)}) copy-start(f32[2048]{0:T(1024)S(1)} %fusion.70) | copy-start | bytes 24580
  515.2 46.6 %copy-start.63 = (f32[512]{0:T(512)S(1)}, f32[512]{0:T(512)}, u32[]{:S(2)}) copy-start(f32[512]{0:T(512)} %convert_element_type.163) | copy-start | bytes 6148
  561.8 11.2 copy-start.8
  561.8 11.2 copy-start.43
  561.8 11.2 copy-start.44
  573.0 4.7 copy-start.5
  605.2 12.9 copy-start.40
  605.2 13.0 copy-start.11
  619.7 4.3 copy-start.36
  629.0 7.2 copy-start.2
  629.0 7.2 copy-start.21
  629.0 7.2 copy-start.22
  629.0 7.2 copy-start.34
  636.4 6.8 copy-start.4
  726.5 10.9 copy-start
  737.5 6.3 copy-start.3
  745.7 6.8 copy-start.4
  837.0 10.9 copy-start
  847.9 7.6 copy-start.3
  857.5 6.8 copy-start.4
  948.8 10.9 copy-start
  959.7 7.6 copy-start.3
  969.3 6.8 copy-start.4
  1060.6 10.9 copy-start
  1071.5 7.6 copy-start.3
  1085.0 4.7 copy-start.9
  1085.0 263.4 %reduce-scatter.16.cloned.1.call-start = ((), (), s32[]{:S(2)}) async-start(), calls=%async_computation.10 | async-start | bytes 1081344 | tf_op jit(solution)/shard_map/reduce_scatter | solution.py:294
  1089.7 392.1 %reduce-scatter.22.cloned.1.call-start = ((), (), s32[]{:S(2)}) async-start(), calls=%async_computation.13 | async-start | bytes 1081344
  1089.7 3.7 copy-start.27
  1096.0 519.3 %reduce-scatter.24.cloned.1.call-start = ((), (), s32[]{:S(2)}) async-start(), calls=%async_computation.14 | async-start | bytes 1081344
  1096.0 4.0 copy-start.28
  1102.9 645.9 %reduce-scatter.26.cloned.1.call-start = ((), (), s32[]{:S(2)}) async-start(), calls=%async_computation.15 | async-start | bytes 1081344
  1103.0 4.0 copy-start.29
  1109.9 778.6 %reduce-scatter.18.cloned.1.call-start = ((), (), s32[]{:S(2)}) async-start(), calls=%async_computation.11 | async-start | bytes 4325376 | tf_op jit(solution)/shard_map/reduce_scatter | solution.py:298
  1121.2 907.0 %reduce-scatter.20.cloned.1.call-start = ((), (), s32[]{:S(2)}) async-start(), calls=%async_computation.12 | async-start | bytes 4325376 | tf_op jit(solution)/shard_map/reduce_scatter | solution.py:300
  1132.1 4.5 copy-start.20
  1136.1 3.5 copy-start.33
  1136.6 4.3 copy-start.38
  1146.0 5.4 copy-start.50
  1146.0 5.4 copy-start.51
  1146.0 5.4 copy-start.52
  1146.0 5.4 copy-start.53
  1146.0 5.4 copy-start.55
  1146.0 5.4 copy-start.59
  1146.1 5.4 copy-start.60
  (19 other events, 37.3 us)
Sparse Core Ops, SparseCore 0:
  10.9 59.0 all-gather.2
  72.9 55.6 all-gather.4
  1085.1 129.7 reduce-scatter.13
  1217.6 130.6 reduce-scatter.15
  1351.0 130.7 reduce-scatter.21
  1484.5 130.6 reduce-scatter.23
  1618.1 130.7 reduce-scatter.25
  1751.8 136.6 reduce-scatter.17
  1891.5 136.7 reduce-scatter.19
where the time goes:
time: 2040 us
  waiting for transfers between devices  836 us (41%)
  matrix products  603 us (30%)
  blocking collectives  279 us (14%)
  other arithmetic  207 us (10%)
  local copies, waits for them, and re-layouts  92.5 us (5%)
    unnamed x12, waiting for transfers between devices  402 us
    dot_general x8, matrix products, score_block(): jnp.einsum('qhd,khd->hqk', query_block, key_heads, preferred_element_type...  158 us
    reduce_scatter x1, waiting for transfers between devices, shards(): lax.psum_scatter(grad_down, 'dp', scatter_dimension=0, tiled=True)  140 us
    reduce_scatter x1, waiting for transfers between devices, shards(): lax.psum_scatter(grad_up, 'dp', scatter_dimension=0, tiled=True)  140 us
    reduce_scatter x1, waiting for transfers between devices, shards(): lax.psum_scatter(grad_out, 'dp', scatter_dimension=0, tiled=True)  133 us
    convert_element_type x4, other arithmetic, backward_block(): (tok_probs * (tok_dprobs - centre[..., None])).astype(jnp.bfloat16)  110 us
    unnamed x2, blocking collectives  79.6 us
    dot_general x8, matrix products, matmul(): return jnp.dot(left, right, preferred_element_type=jnp.float32)  69.4 us
  transfers between devices with their start and end apart: 9, of which 7 were waited for; matrix products, arithmetic and copies ran while one was open for 18% of the time, Pallas kernels for 0%

commit v1 on v0

--- a/solution.py
+++ b/solution.py
@@ -8,6 +8,27 @@
 QB = 512
 EPS = 1e-05
 NEG = -1e30
+
+
+def time_numbers_on_mesh(inner_x, dimension_no):
+    arr_out = list(inner_x.shape[1:])
+    arr_out[dimension_no] *= inner_x.shape[0]
+    return jnp.moveaxis(inner_x, 0, dimension_no).reshape(arr_out)
+
+
+def derive_table_here(own_rows, along_axis):
+    arr_now = own_rows[None]
+    degree = lax.axis_size(along_axis)
+    for num in range(degree.bit_length() - 1):
+        local_part = 1 << num
+        right_arr = lax.ppermute(
+            arr_now, axis_name=along_axis, perm=[(jj, jj ^ local_part) for jj in range(degree)]
+        )
+        long_array = jnp.stack([arr_now, right_arr])
+        aux = lax.axis_index(along_axis)
+        x_next = aux >> num & 1
+        arr_now = jnp.where(x_next == 0, long_array, long_array[::-1]).reshape(-1, *own_rows.shape)
+    return arr_now
 
 
 def normalize(value, gain):
@@ -63,6 +84,11 @@
     shift_ffn,
     cotangent,
 ):
+
+    def choose_wires(xin, my_data, where_dim):
+        u1 = derive_table_here(xin, my_data)
+        return time_numbers_on_mesh(u1, where_dim)
+
     full = (
         lax.all_gather(memory, "dp", axis=1, tiled=True),
         lax.all_gather(w_query, "dp", axis=0, tiled=True),
@@ -70,7 +96,7 @@
         lax.all_gather(w_key, "dp", axis=0, tiled=True),
         lax.all_gather(w_value, "dp", axis=0, tiled=True),
         lax.all_gather(b_value, "dp", axis=0, tiled=True),
-        lax.all_gather(w_out, "dp", axis=0, tiled=True),
+        choose_wires(w_out, my_data="dp", where_dim=0),
         lax.all_gather(b_out, "dp", axis=0, tiled=True),
         lax.all_gather(gain_attn, "dp", axis=0, tiled=True),
         lax.all_gather(shift_attn, "dp", axis=0, tiled=True),

time: 2040 us -> 2050 us (level)
    unnamed x161 -> x169, local copies, waits for them, and re-layouts: 52.6 us -> 53.1 us
  transfers between devices with their start and end apart: 9 -> 14, of which waited for: 7 -> 8; matrix products, arithmetic and copies ran while one was open for 18% -> 18% of each run, Pallas kernels for 0% -> 0%
where the time goes in v1:
time: 2050 us; the launch traced here: 2040 us
  waiting for transfers between devices  836 us (41%)
  matrix products  602 us (29%)
  blocking collectives  284 us (14%)
  other arithmetic  207 us (10%)
  local copies, waits for them, and re-layouts  92.2 us (4%)
    unnamed x12, waiting for transfers between devices  401 us
    dot_general x8, matrix products, score_block(): jnp.einsum('qhd,khd->hqk', query_block, key_heads, preferred_element_type...  158 us
    reduce_scatter x1, waiting for transfers between devices, shards(): lax.psum_scatter(grad_up, 'dp', scatter_dimension=0, tiled=True)  140 us
    reduce_scatter x1, waiting for transfers between devices, shards(): lax.psum_scatter(grad_down, 'dp', scatter_dimension=0, tiled=True)  140 us
    reduce_scatter x1, waiting for transfers between devices, shards(): lax.psum_scatter(grad_out, 'dp', scatter_dimension=0, tiled=True)  134 us
    convert_element_type x4, other arithmetic, backward_block(): (tok_probs * (tok_dprobs - centre[..., None])).astype(jnp.bfloat16)  110 us
    unnamed x2, blocking collectives  79.6 us
    dot_general x8, matrix products, matmul(): return jnp.dot(left, right, preferred_element_type=jnp.float32)  68 us
  transfers between devices with their start and end apart: 14, of which 8 were waited for; matrix products, arithmetic and copies ran while one was open for 18% of the time, Pallas kernels for 0%

profile of v1, /device:TPU:0, one launch (start us, length us, event | category | flops | bytes accessed | tf_op | source)
XLA Modules:
  0.0 2042.5 jit_solution(321302888856562831)
XLA Ops:
  16.4 42.2 %all-reduce.19 = (bf16[512]{0:T(512)(128)(2,1)S(1)}, bf16[512]{0:T(512)(128)(2,1)S(1)}, bf16[512]{0:T(512)(128)(2,1)}, bf16[512]{0:T(512)(128)(2,1)}, bf16[512]{...) all-reduce(bf16[512]{0:T(512)(128)(2,1)S(1)} %dynamic-update-slice,, ...), channel_id=1, replica_groups=mesh['dp'=32] {'dp'}, use_global_device_ids=true, to_apply=%add | all-reduce | flops 6144 | bytes 24576
  58.6 41.4 %all_gather.59 = bf16[20,512]{0,1:T(8,128)(2,1)S(1)} all-gather(bf16[20,16]{0,1:T(8,128)(2,1)} %param.27), channel_id=1, replica_groups=mesh['dp'=32] {'dp'}, dimensions={1}, use_global_device_ids=true | all-gather | bytes 21120 | tf_op jit(solution)/shard_map/all_gather | solution.py:93
  100.0 38.8 %all_gather.58 = bf16[512,512]{1,0:T(8,128)(2,1)S(1)} all-gather(bf16[16,512]{1,0:T(8,128)(2,1)} %param.30), channel_id=1, replica_groups=mesh['dp'=32] {'dp'}, dimensions={0}, use_global_device_ids=true | all-gather | bytes 540672 | tf_op jit(solution)/shard_map/all_gather | solution.py:96
  138.8 39.7 %all_gather.60 = bf16[512,512]{1,0:T(8,128)(2,1)S(1)} all-gather(bf16[16,512]{1,0:T(8,128)(2,1)} %param.31), channel_id=1, replica_groups=mesh['dp'=32] {'dp'}, dimensions={0}, use_global_device_ids=true | all-gather | bytes 540672 | tf_op jit(solution)/shard_map/all_gather | solution.py:97
  178.5 38.3 %all_gather.56 = bf16[512,512]{1,0:T(8,128)(2,1)S(1)} all-gather(bf16[16,512]{1,0:T(8,128)(2,1)} %param.28), channel_id=1, replica_groups=mesh['dp'=32] {'dp'}, dimensions={0}, use_global_device_ids=true | all-gather | bytes 540672 | tf_op jit(solution)/shard_map/all_gather | solution.py:94
  232.3 6.3 reshape.301
  238.6 5.4 copy.82
  246.3 207.4 %while.31 = (s32[]{:T(128)}, bf16[4,512,8,64]{1,3,2,0:T(8,128)(2,1)}, f32[4,8,512]{2,1,0:T(8,128)}, s32[2048]{0:T(1024)}, s32[4,512]{1,0:T(4,128)}, /*index=5*/b...) while((s32[]{:T(128)}, ...), condition=%wide.region_5.6_spmd, body=%wide.region_0.5_spmd.sunk | while | flops 2271260672 | bytes 114112640 | solution.py:182
  249.6 14.7 fusion.190
  264.4 15.0 fusion.192
  280.1 15.7 fusion.194
  301.5 14.7 fusion.190
  316.3 15.0 fusion.192
  331.9 15.7 fusion.194
  353.3 14.7 fusion.190
  368.2 15.0 fusion.192
  383.8 15.7 fusion.194
  405.2 14.7 fusion.190
  420.0 15.0 fusion.192
  435.6 15.7 fusion.194
  471.2 46.0 %all_gather.71 = bf16[512,512]{1,0:T(8,128)(2,1)} all-gather(bf16[16,512]{1,0:T(8,128)(2,1)S(1)} %copy-done.43), channel_id=1, replica_groups=mesh['dp'=32] {'dp'}, dimensions={0}, use_global_device_ids=true | all-gather | bytes 540672 | tf_op jit(solution)/shard_map/all_gather | solution.py:199
  522.1 46.5 %multiply_convert_fusion.2 = (bf16[2048,2048]{1,0:T(8,128)(2,1)}, f32[2048,2048]{1,0:T(8,128)}, f32[2048,2048]{1,0:T(8,128)}) fusion(f32[2048]{0:T(1024)S(1)} %convert_element_type.161, bf16[512,2048]{1,0:T(8,128)(2,1)} %all-gather.3.cloned.1.call-done, f32[2048,512]{0,1:T(8,128)} %copy-done.10, f32[512]{0:T(512)S(1)} %convert_element_type.159, ...), kind=kOutput, calls=%fused_computation.84 | convolution fusion | flops 4577034240 | bytes 48263168 | tf_op jit(solution)/shard_map/dot_general | solution.py:46
  568.7 11.1 fusion.83
  584.5 4.8 convert_reduce_fusion.1
  589.3 22.8 %convert_reduce_fusion = (f32[2048]{0:T(1024)}, bf16[2048,2048]{1,0:T(8,128)(2,1)}) fusion(f32[2048,2048]{1,0:T(8,128)} %get-tuple-element.425, bf16[2048,512]{0,1:T(8,128)(2,1)} %get-tuple-element.415, bf16[2048,512]{1,0:T(8,128)(2,1)} %all-gather.5.cloned.1.call-done, f32[2048,2048]{1,0:T(8,128)} %get-tuple-element.441, f32[2048]{0:T(1024)S(1)} %convert_element_type.161), kind=kOutput, calls=%fused_computation.82 | convolution fusion | flops 4366268416 | bytes 46153728 | tf_op jit(solution)/shard_map/dot_general | solution.py:56
  612.0 12.9 multiply_reduce_fusion.3
  635.8 5.6 copy.90
  643.0 445.6 %while.32 = (s32[]{:T(128)}, f32[2048,8,64]{0,2,1:T(8,128)}, f32[2048,8,64]{0,2,1:T(8,128)}, f32[20,8,64]{2,0,1:T(8,128)S(1)}, f32[20,8,64]{2,0,1:T(8,128)S(1)},...) while((s32[]{:T(128)}, f32[2048,8,64]{0,2,1:T(8,128)}, ...), condition=%wide.region_17.18_spmd.clone, body=%wide.region_14.17_spmd.clone.sunk | while | flops 5504415744 | bytes 366266624 | solution.py:295
  650.0 14.2 fusion.214
  664.2 24.7 %multiply_reduce_fusion.10 = (f32[8,512]{1,0:T(8,128)S(1)}, f32[8,512,2048]{2,1,0:T(8,128)}) fusion(f32[8,512,2048]{2,1,0:T(8,128)} %fusion.214, f32[8,512]{1,0:T(8,128)S(1)} %dynamic-slice_bitcast_fusion.2, bf16[2048,8,64]{0,2,1:T(8,128)(2,1)S(1)} %get-tuple-element.695, bf16[4,512,8,64]{1,3,2,0:T(8,128)(2,1)} %get-tuple-element.692, ...), kind=kOutput, calls=%fused_computation.29.clone.1 | convolution fusion | flops 1115680768 | bytes 70811648 | tf_op jit(solution)/shard_map/while/body/eval_jaxpr/qhd,khd->hqk/dot_general | solution.py:153
  688.9 27.5 %multiply_convert_fusion.5 = bf16[8,512,2048]{2,1,0:T(8,128)(2,1)} fusion(f32[8,512,2048]{2,1,0:T(8,128)} %get-tuple-element.615, f32[8,512,2048]{2,1,0:T(8,128)} %fusion.214, f32[8,512]{1,0:T(8,128)S(1)} %add.399), kind=kLoop, calls=%fused_computation.28.clone.1 | loop fusion | flops 25165824 | bytes 83902464 | tf_op jit(solution)/shard_map/while/body/eval_jaxpr/convert_element_type | solution.py:251
  716.4 15.7 bitcast_add_fusion.5
  733.4 9.9 fusion.218
  744.4 6.3 bitcast_add_fusion.4
  759.4 14.2 fusion.214
  773.6 24.7 %multiply_reduce_fusion.10 = (f32[8,512]{1,0:T(8,128)S(1)}, f32[8,512,2048]{2,1,0:T(8,128)}) fusion(f32[8,512,2048]{2,1,0:T(8,128)} %fusion.214, f32[8,512]{1,0:T(8,128)S(1)} %dynamic-slice_bitcast_fusion.2, bf16[2048,8,64]{0,2,1:T(8,128)(2,1)S(1)} %get-tuple-element.695, bf16[4,512,8,64]{1,3,2,0:T(8,128)(2,1)} %get-tuple-element.692, ...), kind=kOutput, calls=%fused_computation.29.clone.1 | convolution fusion | flops 1115680768 | bytes 70811648 | tf_op jit(solution)/shard_map/while/body/eval_jaxpr/qhd,khd->hqk/dot_general | solution.py:153
  798.3 27.5 %multiply_convert_fusion.5 = bf16[8,512,2048]{2,1,0:T(8,128)(2,1)} fusion(f32[8,512,2048]{2,1,0:T(8,128)} %get-tuple-element.615, f32[8,512,2048]{2,1,0:T(8,128)} %fusion.214, f32[8,512]{1,0:T(8,128)S(1)} %add.399), kind=kLoop, calls=%fused_computation.28.clone.1 | loop fusion | flops 25165824 | bytes 83902464 | tf_op jit(solution)/shard_map/while/body/eval_jaxpr/convert_element_type | solution.py:251
  825.8 16.9 bitcast_add_fusion.5
  844.1 9.9 fusion.218
  855.0 7.6 bitcast_add_fusion.4
  871.4 14.2 fusion.214
  885.5 24.7 %multiply_reduce_fusion.10 = (f32[8,512]{1,0:T(8,128)S(1)}, f32[8,512,2048]{2,1,0:T(8,128)}) fusion(f32[8,512,2048]{2,1,0:T(8,128)} %fusion.214, f32[8,512]{1,0:T(8,128)S(1)} %dynamic-slice_bitcast_fusion.2, bf16[2048,8,64]{0,2,1:T(8,128)(2,1)S(1)} %get-tuple-element.695, bf16[4,512,8,64]{1,3,2,0:T(8,128)(2,1)} %get-tuple-element.692, ...), kind=kOutput, calls=%fused_computation.29.clone.1 | convolution fusion | flops 1115680768 | bytes 70811648 | tf_op jit(solution)/shard_map/while/body/eval_jaxpr/qhd,khd->hqk/dot_general | solution.py:153
  910.3 27.5 %multiply_convert_fusion.5 = bf16[8,512,2048]{2,1,0:T(8,128)(2,1)} fusion(f32[8,512,2048]{2,1,0:T(8,128)} %get-tuple-element.615, f32[8,512,2048]{2,1,0:T(8,128)} %fusion.214, f32[8,512]{1,0:T(8,128)S(1)} %add.399), kind=kLoop, calls=%fused_computation.28.clone.1 | loop fusion | flops 25165824 | bytes 83902464 | tf_op jit(solution)/shard_map/while/body/eval_jaxpr/convert_element_type | solution.py:251
  937.7 16.9 bitcast_add_fusion.5
  956.0 9.9 fusion.218
  966.9 7.6 bitcast_add_fusion.4
  983.3 14.2 fusion.214
  997.5 24.7 %multiply_reduce_fusion.10 = (f32[8,512]{1,0:T(8,128)S(1)}, f32[8,512,2048]{2,1,0:T(8,128)}) fusion(f32[8,512,2048]{2,1,0:T(8,128)} %fusion.214, f32[8,512]{1,0:T(8,128)S(1)} %dynamic-slice_bitcast_fusion.2, bf16[2048,8,64]{0,2,1:T(8,128)(2,1)S(1)} %get-tuple-element.695, bf16[4,512,8,64]{1,3,2,0:T(8,128)(2,1)} %get-tuple-element.692, ...), kind=kOutput, calls=%fused_computation.29.clone.1 | convolution fusion | flops 1115680768 | bytes 70811648 | tf_op jit(solution)/shard_map/while/body/eval_jaxpr/qhd,khd->hqk/dot_general | solution.py:153
  1022.2 27.5 %multiply_convert_fusion.5 = bf16[8,512,2048]{2,1,0:T(8,128)(2,1)} fusion(f32[8,512,2048]{2,1,0:T(8,128)} %get-tuple-element.615, f32[8,512,2048]{2,1,0:T(8,128)} %fusion.214, f32[8,512]{1,0:T(8,128)S(1)} %add.399), kind=kLoop, calls=%fused_computation.28.clone.1 | loop fusion | flops 25165824 | bytes 83902464 | tf_op jit(solution)/shard_map/while/body/eval_jaxpr/convert_element_type | solution.py:251
  1049.6 16.9 bitcast_add_fusion.5
  1067.9 9.9 fusion.218
  1078.8 7.6 bitcast_add_fusion.4
  1092.3 4.6 fusion.88
  1117.4 11.2 fusion.74
  1128.9 10.6 fusion.89
  1153.5 5.3 copy.100
  1158.9 37.3 %all-reduce.18 = (f32[512]{0:T(512)S(1)}, f32[512]{0:T(512)S(1)}, f32[512]{0:T(512)S(1)}, f32[512]{0:T(512)S(1)}, f32[512]{0:T(512)S(1)}, /*index=5*/f32[2048]{0...) all-reduce(f32[512]{0:T(512)S(1)} %reduce_sum.215, ...), channel_id=4, replica_groups=mesh['dp'=32] {'dp'}, use_global_device_ids=true, to_apply=%region_21.22.clone | all-reduce | flops 6144 | bytes 49152
  1201.4 20.6 %reduce-scatter.14.cloned.1.call-done = f32[20,16]{0,1:T(8,128)} async-done(((f32[20,512]{0,1:T(8,128)}), f32[20,16]{0,1:T(8,128)}) %reduce-scatter.14.cloned.1.call-update) | async-done | bytes 1296 | tf_op jit(solution)/shard_map/reduce_scatter | solution.py:314
  1222.0 133.5 %reduce-scatter.16.cloned.1.call-done = f32[16,512]{1,0:T(8,128)} async-done(((f32[512,512]{1,0:T(8,128)}), f32[16,512]{1,0:T(8,128)}) %reduce-scatter.16.cloned.1.call-update) | async-done | bytes 32784 | tf_op jit(solution)/shard_map/reduce_scatter | solution.py:320
  1355.6 133.4 %reduce-scatter.22.cloned.1.call-done = f32[16,512]{1,0:T(8,128)} async-done(((f32[512,512]{1,0:T(8,128)}), f32[16,512]{1,0:T(8,128)}) %reduce-scatter.22.cloned.1.call-update) | async-done | bytes 32784
  1489.0 133.5 %reduce-scatter.24.cloned.1.call-done = f32[16,512]{1,0:T(8,128)} async-done(((f32[512,512]{1,0:T(8,128)}), f32[16,512]{1,0:T(8,128)}) %reduce-scatter.24.cloned.1.call-update) | async-done | bytes 32784
  1622.5 133.5 %reduce-scatter.26.cloned.1.call-done = f32[16,512]{1,0:T(8,128)} async-done(((f32[512,512]{1,0:T(8,128)}), f32[16,512]{1,0:T(8,128)}) %reduce-scatter.26.cloned.1.call-update) | async-done | bytes 32784
  1756.0 139.8 %reduce-scatter.18.cloned.1.call-done = f32[16,2048]{1,0:T(8,128)} async-done(((f32[512,2048]{1,0:T(8,128)}), f32[16,2048]{1,0:T(8,128)}) %reduce-scatter.18.cloned.1.call-update) | async-done | bytes 131088 | tf_op jit(solution)/shard_map/reduce_scatter | solution.py:324
  1895.9 139.6 %reduce-scatter.20.cloned.1.call-done = f32[64,512]{1,0:T(8,128)} async-done(((f32[2048,512]{1,0:T(8,128)}), f32[64,512]{1,0:T(8,128)}) %reduce-scatter.20.cloned.1.call-update) | async-done | bytes 131088 | tf_op jit(solution)/shard_map/reduce_scatter | solution.py:326
  (366 shorter events, 178.9 us)
Async XLA Ops:
  7.2 515.0 %all-gather.3.cloned.1.call-start = ((), (), s32[]{:S(2)}) async-start(), calls=%async_computation.7 | async-start | bytes 2162688 | tf_op jit(solution)/shard_map/all_gather | solution.py:103
  7.9 560.8 %all-gather.5.cloned.1.call-start = ((), (), s32[]{:S(2)}) async-start(), calls=%async_computation.8 | async-start | bytes 2162688 | tf_op jit(solution)/shard_map/all_gather | solution.py:105
  8.0 217.5 %collective-permute-start = (bf16[1,16,512]{2,1,0:T(8,128)(2,1)}, bf16[1,16,512]{2,1,0:T(8,128)(2,1)S(1)}, u32[]{:S(2)}, u32[]{:S(2)}) collective-permute-start(bf16[1,16,512]{2,1,0:T(8,128)(2,1)} %bitcast.253), channel_id=1, source_target_pairs={{0,1},{1,0},{2,3},{3,2},{4,5},{5,4},{6,7},{7,6},{8,9},{9,8},{10,11... | collective-permute-start | bytes 49160 | tf_op jit(solution)/shard_map/ppermute | solution.py:24
  8.7 1213.4 %reduce-scatter.14.cloned.1.call-start = ((), (), s32[]{:S(2)}) async-start(), calls=%async_computation.9 | async-start | bytes 270336 | tf_op jit(solution)/shard_map/reduce_scatter | solution.py:314
  100.0 127.2 %copy-start.23 = (bf16[20,512]{0,1:T(8,128)(2,1)}, bf16[20,512]{0,1:T(8,128)(2,1)S(1)}, u32[]{:S(2)}) copy-start(bf16[20,512]{0,1:T(8,128)(2,1)S(1)} %all_gather.59) | copy-start | bytes 61444
  138.8 88.4 %copy-start.19 = (bf16[512,512]{1,0:T(8,128)(2,1)}, bf16[512,512]{1,0:T(8,128)(2,1)S(1)}, u32[]{:S(2)}) copy-start(bf16[512,512]{1,0:T(8,128)(2,1)S(1)} %all_gather.58) | copy-start | bytes 1572868
  178.5 46.8 %copy-start.13 = (bf16[512,512]{1,0:T(8,128)(2,1)}, bf16[512,512]{1,0:T(8,128)(2,1)S(1)}, u32[]{:S(2)}) copy-start(bf16[512,512]{1,0:T(8,128)(2,1)S(1)} %all_gather.60) | copy-start | bytes 1572868
  222.5 7.1 copy-start.46
  225.5 4.0 collective-permute-start.1
  229.5 14.5 collective-permute-start.2
  244.7 209.1 %collective-permute-start.3 = (bf16[8,16,512]{2,1,0:T(8,128)(2,1)}, bf16[8,16,512]{2,1,0:T(8,128)(2,1)}, u32[]{:S(2)}, u32[]{:S(2)}) collective-permute-start(bf16[8,16,512]{2,1,0:T(8,128)(2,1)} %bitcast.18), channel_id=1, source_target_pairs={{0,8},{1,9},{2,10},{3,11},{4,12},{5,13},{6,14},{7,15},{8,0},{9,1},... | collective-permute-start | bytes 393224 | tf_op jit(solution)/shard_map/ppermute | solution.py:24
  453.7 13.5 copy-start.1
  453.7 7.4 copy-start.68
  453.7 7.4 copy-start.67
  453.7 8.0 copy-start.66
  453.7 8.0 copy-start.65
  453.8 8.0 copy-start.64
  453.8 8.6 copy-start.63
  453.8 9.2 copy-start.57
  455.2 61.9 %collective-permute-start.4 = (bf16[16,16,512]{2,1,0:T(8,128)(2,1)S(1)}, bf16[16,16,512]{2,1,0:T(8,128)(2,1)S(1)}, u32[]{:S(2)}, u32[]{:S(2)}) collective-permute-start(bf16[16,16,512]{2,1,0:T(8,128)(2,1)S(1)} %bitcast.245), channel_id=1, source_target_pairs={{0,16},{1,17},{2,18},{3,19},{4,20},{5,21},{6,22},{7,23},{8,24},{9,... | collective-permute-start | bytes 786440 | tf_op jit(solution)/shard_map/ppermute | solution.py:24
  461.2 163.8 %copy-start.55 = (f32[512]{0:T(512)}, f32[512]{0:T(512)S(1)}, u32[]{:S(2)}) copy-start(f32[512]{0:T(512)S(1)} %convert_element_type.158) | copy-start | bytes 6148
  461.8 106.9 %copy-start.60 = (f32[512]{0:T(512)}, f32[512]{0:T(512)S(1)}, u32[]{:S(2)}) copy-start(f32[512]{0:T(512)S(1)} %convert_element_type.159) | copy-start | bytes 6148
  470.5 46.8 %copy-start.31 = (bf16[2048,512]{0,1:T(8,128)(2,1)S(1)}, bf16[2048,512]{0,1:T(8,128)(2,1)}, u32[]{:S(2)}) copy-start(bf16[2048,512]{0,1:T(8,128)(2,1)} %copy.80) | copy-start | bytes 6291460
  471.2 47.8 %copy-start.30 = (bf16[64,8,4,512]{3,1,2,0:T(8,128)(2,1)}, bf16[64,8,4,512]{3,1,2,0:T(8,128)(2,1)S(1)}, u32[]{:S(2)}) copy-start(bf16[64,8,4,512]{3,1,2,0:T(8,128)(2,1)S(1)} %copy.118) | copy-start | bytes 6291460
  519.0 106.0 %copy-start.40 = (f32[2048]{0:T(1024)}, f32[2048]{0:T(1024)S(1)}, u32[]{:S(2)}) copy-start(f32[2048]{0:T(1024)S(1)} %broadcast_multiply_fusion.1) | copy-start | bytes 24580
  522.1 102.9 %copy-start.47 = (f32[2048]{0:T(1024)}, f32[2048]{0:T(1024)S(1)}, u32[]{:S(2)}) copy-start(f32[2048]{0:T(1024)S(1)} %fusion.72) | copy-start | bytes 24580
  522.1 46.6 %copy-start.62 = (f32[512]{0:T(512)S(1)}, f32[512]{0:T(512)}, u32[]{:S(2)}) copy-start(f32[512]{0:T(512)} %convert_element_type.163) | copy-start | bytes 6148
  568.7 11.2 copy-start.8
  568.7 11.2 copy-start.44
  568.7 11.2 copy-start.45
  579.8 4.7 copy-start.5
  612.0 12.9 copy-start.39
  612.0 13.0 copy-start.11
  635.8 7.2 copy-start.2
  635.8 7.2 copy-start.21
  635.8 7.2 copy-start.22
  635.8 7.2 copy-start.34
  643.2 6.8 copy-start.4
  733.4 10.9 copy-start
  744.4 6.3 copy-start.3
  752.6 6.8 copy-start.4
  844.1 10.9 copy-start
  855.0 7.6 copy-start.3
  864.6 6.8 copy-start.4
  956.0 10.9 copy-start
  966.9 7.6 copy-start.3
  976.5 6.8 copy-start.4
  1067.9 10.9 copy-start
  1078.8 7.6 copy-start.3
  1092.3 4.8 copy-start.9
  1092.3 263.3 %reduce-scatter.16.cloned.1.call-start = ((), (), s32[]{:S(2)}) async-start(), calls=%async_computation.10 | async-start | bytes 1081344 | tf_op jit(solution)/shard_map/reduce_scatter | solution.py:320
  1097.0 392.0 %reduce-scatter.22.cloned.1.call-start = ((), (), s32[]{:S(2)}) async-start(), calls=%async_computation.13 | async-start | bytes 1081344
  1103.3 519.2 %reduce-scatter.24.cloned.1.call-start = ((), (), s32[]{:S(2)}) async-start(), calls=%async_computation.14 | async-start | bytes 1081344
  1110.3 645.8 %reduce-scatter.26.cloned.1.call-start = ((), (), s32[]{:S(2)}) async-start(), calls=%async_computation.15 | async-start | bytes 1081344
  1117.3 778.6 %reduce-scatter.18.cloned.1.call-start = ((), (), s32[]{:S(2)}) async-start(), calls=%async_computation.11 | async-start | bytes 4325376 | tf_op jit(solution)/shard_map/reduce_scatter | solution.py:324
  1128.6 906.9 %reduce-scatter.20.cloned.1.call-start = ((), (), s32[]{:S(2)}) async-start(), calls=%async_computation.12 | async-start | bytes 4325376 | tf_op jit(solution)/shard_map/reduce_scatter | solution.py:326
  1139.5 4.5 copy-start.20
  1153.4 5.4 copy-start.49
  1153.4 5.4 copy-start.50
  1153.4 5.4 copy-start.51
  1153.4 5.4 copy-start.52
  1153.4 5.4 copy-start.54
  1153.4 5.4 copy-start.58
  1153.5 5.4 copy-start.59
  (28 other events, 72.5 us)
Sparse Core Ops, SparseCore 0:
  10.9 59.2 all-gather.2
  73.0 55.7 all-gather.4
  1092.4 129.5 reduce-scatter.13
  1224.8 130.7 reduce-scatter.15
  1358.2 130.7 reduce-scatter.21
  1491.8 130.7 reduce-scatter.23
  1625.3 130.6 reduce-scatter.25
  1759.0 136.8 reduce-scatter.17
  1898.8 136.6 reduce-scatter.19
